TPU v7x, 256 devices: a whole 4x4x8 slice. The times are simulated.
256 devices in a mesh: dp: 16 (over y, x), tensor: 16 (over z, core).
Axes of the slice: x: 4, y: 4, z: 8, core: 2. Of those that a mesh axis runs over, the one named last changes fastest.
Arguments:
- tokens: bfloat16 [4096, 6144], P('dp'), may hold values from -6 to 6
- target: bfloat16 [4096, 6144], P('dp'), may hold values from -6 to 6
- pair_bias: float32 [4096, 32, 256], P('dp', 'tensor'), may hold values from -6 to 680
- neighbours: int32 [4096, 256], P('dp'), may hold values 0 or 1
- w_query: bfloat16 [6144, 4096], P('dp', 'tensor'), may hold values from -0.078125 to 0.078125
- w_key: bfloat16 [6144, 4096], P('dp', 'tensor'), may hold values from -0.078125 to 0.078125
- w_value: bfloat16 [6144, 4096], P('dp', 'tensor'), may hold values from -0.078125 to 0.078125
- w_out: bfloat16 [4096, 6144], P('tensor', 'dp'), may hold values from -0.09375 to 0.09375
- basis_value: float32 [6144, 4096], P('dp', 'tensor'), may hold values from -32 to 32
- basis_out: float32 [4096, 6144], P('tensor', 'dp'), may hold values from -32 to 32
- prior_value: float32 [6144, 4096], P('dp', 'tensor'), may hold values from -32 to 32
- prior_out: float32 [4096, 6144], P('tensor', 'dp'), may hold values from -32 to 32
- prior_beta: float32 [], replicated, may hold values from 10 to 60
Outputs:
- next_value: float32 [6144, 4096], P('dp', 'tensor')
- next_out: float32 [4096, 6144], P('tensor', 'dp')
- coefficients: float32 [2], replicated
All inputs are finite; a program needn't handle non-finite values. No bound on the sum of `neighbours` on one device may be relied on, other than what follows from the above.
Results may differ from a plain program's by a relative error of at most 0.02.
Values may be sent and summed in bfloat16 or wider, within the bound.
A program may use at most 128 MiB of HBM per device.

v0:
```python
import math
import jax
import jax.numpy as jnp
from jax import lax
from jax.sharding import PartitionSpec as P

HEAD_DIM = 128
loss_gain = 32.0
epsilon = 1e-06


def body(
    tokens,
    target,
    pair_bias,
    neighbours,
    w_query,
    w_key,
    w_value,
    w_out,
    basis_value,
    basis_out,
    prior_value,
    prior_out,
    prior_beta,
):
    count = tokens.shape[0]
    features = tokens.shape[1]
    local_width = w_query.shape[1]
    heads_here = local_width // HEAD_DIM
    full_width = local_width * lax.axis_size("tensor")
    groups = lax.axis_size("dp")
    total_tokens = count * groups
    xf = tokens.astype(jnp.float32)
    normed = (xf * lax.rsqrt(jnp.mean(xf * xf, axis=1, keepdims=True) + epsilon)).astype(
        jnp.bfloat16
    )
    basis_value_b = basis_value.astype(jnp.bfloat16)
    pieces = (
        lax.all_gather(w_query, "dp", axis=0, tiled=True),
        lax.all_gather(w_key, "dp", axis=0, tiled=True),
        lax.all_gather(w_value, "dp", axis=0, tiled=True),
        lax.all_gather(basis_value_b, "dp", axis=0, tiled=True),
    )
    query_acc, key_acc, value_acc, tangent_acc = tuple(
        (jnp.dot(normed, piece, preferred_element_type=jnp.float32) for piece in pieces)
    )
    shape3 = (count, heads_here, HEAD_DIM)
    query = query_acc.astype(jnp.bfloat16).reshape(shape3)
    keys = key_acc.astype(jnp.bfloat16).reshape(shape3)
    values = value_acc.astype(jnp.bfloat16).reshape(shape3)
    tangent_values = (tangent_acc / math.sqrt(features)).astype(jnp.bfloat16).reshape(shape3)
    out_full, tangent_out = (
        lax.all_gather(w_out, "dp", axis=1, tiled=True),
        lax.all_gather(basis_out.astype(jnp.bfloat16), "dp", axis=1, tiled=True),
    )
    scores = (
        jnp.einsum("thd,shd->ths", query, keys, preferred_element_type=jnp.float32)
        / math.sqrt(HEAD_DIM)
        + pair_bias
    )
    rows = lax.broadcasted_iota(jnp.int32, (count, count), 0)
    cols = lax.broadcasted_iota(jnp.int32, (count, count), 1)
    allowed = (neighbours == 1) | (jnp.abs(rows - cols) <= 1)
    scores = jnp.where(allowed[:, None, :], scores, -jnp.inf)
    probs = jax.nn.softmax(scores, axis=2).astype(jnp.bfloat16)
    mixed = (
        jnp.einsum("ths,shd->thd", probs, values, preferred_element_type=jnp.float32)
        .astype(jnp.bfloat16)
        .reshape(count, local_width)
    )
    tangent_mixed = (
        jnp.einsum("ths,shd->thd", probs, tangent_values, preferred_element_type=jnp.float32)
        .astype(jnp.bfloat16)
        .reshape(count, local_width)
    )
    scale_out = 1.0 / math.sqrt(full_width)
    partial_value = jnp.dot(mixed, out_full, preferred_element_type=jnp.float32)
    tangent_partial = jnp.dot(
        mixed, tangent_out, preferred_element_type=jnp.float32
    ) * scale_out + jnp.dot(tangent_mixed, out_full, preferred_element_type=jnp.float32)
    attn, tangent_attn = (
        lax.psum(partial_value.astype(jnp.bfloat16), "tensor").astype(jnp.float32),
        lax.psum(tangent_partial.astype(jnp.bfloat16), "tensor").astype(jnp.float32),
    )
    factor = loss_gain * full_width / total_tokens
    error = ((xf + attn - target.astype(jnp.float32)) * factor).astype(jnp.bfloat16)
    tangent_error = (tangent_attn * factor).astype(jnp.bfloat16)
    first = jnp.einsum("td,ta->da", error, tangent_mixed, preferred_element_type=jnp.float32)
    second = jnp.einsum("td,ta->da", tangent_error, mixed, preferred_element_type=jnp.float32)
    curv_out = (
        lax.psum_scatter(
            ((first + second) * scale_out).astype(jnp.bfloat16),
            "dp",
            scatter_dimension=0,
            tiled=True,
        )
        .astype(jnp.float32)
        .T
    )
    back_tangent = (
        jnp.einsum("td,ad->ta", tangent_error, out_full, preferred_element_type=jnp.float32)
        + jnp.einsum("td,ad->ta", error, tangent_out, preferred_element_type=jnp.float32)
        * scale_out
    ).astype(jnp.bfloat16)
    value_back = (
        jnp.einsum(
            "ths,thd->shd", probs, back_tangent.reshape(shape3), preferred_element_type=jnp.float32
        )
        .astype(jnp.bfloat16)
        .reshape(count, local_width)
    )
    scale_value = 1.0 / math.sqrt(features)
    curv_value = lax.psum_scatter(
        (
            jnp.einsum("ti,ta->ia", normed, value_back, preferred_element_type=jnp.float32)
            * scale_value
        ).astype(jnp.bfloat16),
        "dp",
        scatter_dimension=0,
        tiled=True,
    ).astype(jnp.float32)
    entries = 2.0 * features * full_width
    alpha = (
        lax.psum(
            jnp.sum(basis_value * curv_value) + jnp.sum(basis_out * curv_out), ("dp", "tensor")
        )
        / entries
    )
    rest_value = curv_value - alpha * basis_value - prior_beta * prior_value
    rest_out = curv_out - alpha * basis_out - prior_beta * prior_out
    squares = (
        lax.psum(jnp.sum(rest_value * rest_value) + jnp.sum(rest_out * rest_out), ("dp", "tensor"))
        / entries
    )
    beta = jnp.sqrt(squares + epsilon)
    return (rest_value / beta, rest_out / beta, jnp.stack([alpha, beta]))


def solution(mesh):
    placed = (
        P("dp", None),
        P("dp", None),
        P("dp", "tensor", None),
        P("dp", None),
        P("dp", "tensor"),
        P("dp", "tensor"),
        P("dp", "tensor"),
        P("tensor", "dp"),
        P("dp", "tensor"),
        P("tensor", "dp"),
        P("dp", "tensor"),
        P("tensor", "dp"),
        P(),
    )
    return jax.shard_map(
        body,
        mesh=mesh,
        in_specs=placed,
        out_specs=(P("dp", "tensor"), P("tensor", "dp"), P()),
        check_vma=False,
    )
```

profile of v0, /device:TPU:1, one launch (start us, length us, event | category | flops | bytes accessed | tf_op | source)
XLA Modules:
  0.0 824.5 jit_solution(4294563663317649409)
XLA Ops:
  7.2 0.7 all-gather.9.cloned.1.call-update
  8.0 0.7 all-gather.11.cloned.1.call-update
  8.7 0.7 all-gather.7.cloned.1.call-update
  9.4 1.7 convert_element_type.88
  11.2 0.5 all-gather.17.cloned.1.call-update
  11.8 1.7 convert_element_type.87
  13.6 2.1 copy.19
  15.7 0.2 copy.16
  15.9 0.7 fusion.5
  16.6 50.3 %all-gather.9.cloned.1.call-done = bf16[6144,256]{1,0:T(8,128)(2,1)} async-done(((bf16[384,256]{1,0:T(8,128)(2,1)}), bf16[6144,256]{1,0:T(8,128)(2,1)}) %all-gather.9.cloned.1.call-update) | async-done | bytes 3145744 | tf_op jit(solution)/shard_map/all_gather | solution.py:41
  66.9 3.4 convolution_convert_fusion.5
  70.4 51.0 %all-gather.11.cloned.1.call-done = bf16[6144,256]{1,0:T(8,128)(2,1)} async-done(((bf16[384,256]{1,0:T(8,128)(2,1)}), bf16[6144,256]{1,0:T(8,128)(2,1)}) %all-gather.11.cloned.1.call-update) | async-done | bytes 3145744 | tf_op jit(solution)/shard_map/all_gather | solution.py:40
  121.3 3.4 convolution_convert_fusion.4
  124.8 2.2 fusion.34
  127.0 1.1 divide_convert_fusion
  128.1 47.7 %all-gather.7.cloned.1.call-done = bf16[6144,256]{1,0:T(8,128)(2,1)} async-done(((bf16[384,256]{1,0:T(8,128)(2,1)}), bf16[6144,256]{1,0:T(8,128)(2,1)}) %all-gather.7.cloned.1.call-update) | async-done | bytes 3145744 | tf_op jit(solution)/shard_map/all_gather | solution.py:42
  175.8 3.4 convolution_convert_fusion.6
  179.2 0.2 convolution_convert_fusion.3
  179.4 51.2 %all-gather.15.cloned.1.call-done = bf16[6144,256]{1,0:T(8,128)(2,1)} async-done(((bf16[384,256]{1,0:T(8,128)(2,1)}), bf16[6144,256]{1,0:T(8,128)(2,1)}) %all-gather.15.cloned.1.call-update) | async-done | bytes 3145744 | tf_op jit(solution)/shard_map/all_gather | solution.py:43
  230.6 3.4 fusion.18
  234.0 0.8 convolution_convert_fusion.2
  234.9 54.0 %all-gather.17.cloned.1.call-done = bf16[256,6144]{1,0:T(8,128)(2,1)} async-done(((bf16[256,384]{1,0:T(8,128)(2,1)}), bf16[256,6144]{1,0:T(8,128)(2,1)}) %all-gather.17.cloned.1.call-update) | async-done | bytes 3145744 | tf_op jit(solution)/shard_map/all_gather | solution.py:54
  288.9 4.5 convolution_convert_fusion
  293.4 55.4 %all-gather.13.cloned.1.call-done = bf16[256,6144]{1,0:T(8,128)(2,1)} async-done(((bf16[256,384]{1,0:T(8,128)(2,1)}), bf16[256,6144]{1,0:T(8,128)(2,1)}) %all-gather.13.cloned.1.call-update) | async-done | bytes 3145744 | tf_op jit(solution)/shard_map/all_gather | solution.py:55
  348.8 3.0 convolution_multiply_fusion.1
  351.9 2.7 fusion.3
  354.6 0.2 reduce-scatter.3.cloned.1.call-start
  354.8 127.6 %all-reduce.3.cloned.1.call-done = (bf16[256,6144]{1,0:T(8,128)(2,1)}, bf16[256,6144]{1,0:T(8,128)(2,1)}) async-done(((bf16[256,6144]{1,0:T(8,128)(2,1)}, bf16[256,6144]{1,0:T(8,128)(2,1)}), (bf16[256,6144]{1,0:T(8,128)(2,1)}, bf16[256,6144]{1,0:T(8,128)(2,1)})) %all-reduce.3.cloned.1.call-update) | async-done | bytes 6291472 | tf_op jit(solution)/shard_map/psum | solution.py:83
  482.4 5.5 convolution_multiply_fusion.3
  488.0 1.0 fusion.17
  489.0 0.2 convolution_convert_fusion.1
  489.2 3.0 fusion.4
  492.3 0.8 copy-done.11
  493.1 5.5 fusion.26
  498.6 3.3 fusion.2
  501.9 1.0 copy-done.8
  503.7 68.5 %reduce-scatter.3.cloned.1.call-done = bf16[384,256]{1,0:T(8,128)(2,1)} async-done(((bf16[6144,256]{1,0:T(8,128)(2,1)}), bf16[384,256]{1,0:T(8,128)(2,1)}) %reduce-scatter.3.cloned.1.call-update) | async-done | bytes 196624 | tf_op jit(solution)/shard_map/reduce_scatter | solution.py:114
  572.2 1.7 fusion.19
  573.9 82.0 %reduce-scatter.5.cloned.1.call-done = bf16[384,256]{1,0:T(8,128)(2,1)} async-done(((bf16[6144,256]{1,0:T(8,128)(2,1)}), bf16[384,256]{1,0:T(8,128)(2,1)}) %reduce-scatter.5.cloned.1.call-update) | async-done | bytes 196624 | tf_op jit(solution)/shard_map/reduce_scatter | solution.py:92
  655.9 1.7 fusion.21
  658.9 0.2 copy.25
  659.1 77.2 %psum.30 = f32[]{:T(128)} all-reduce(f32[]{:T(128)S(6)} %add.54), channel_id=1, replica_groups=mesh['dp'=16,'tensor'=16] {'dp','tensor'}, use_global_device_ids=true, to_apply=%region_9.10 | all-reduce | flops 1 | bytes 8 | tf_op jit(solution)/shard_map/psum | solution.py:125
  736.9 1.6 multiply_reduce_fusion.1
  738.6 1.6 multiply_reduce_fusion
  741.5 73.3 %psum.31 = f32[]{:T(128)} all-reduce(f32[]{:T(128)S(6)} %add.55), channel_id=1, replica_groups=mesh['dp'=16,'tensor'=16] {'dp','tensor'}, use_global_device_ids=true, to_apply=%region_12.13 | all-reduce | flops 1 | bytes 8 | tf_op jit(solution)/shard_map/psum | solution.py:133
  815.6 0.9 copy.26
  816.5 0.6 pad_maximum_fusion
  817.1 0.8 broadcast_divide_fusion.1
  (43 shorter events, 0.8 us)
Async XLA Ops:
  7.2 8.5 %copy-start.13 = (s32[256,256]{1,0:T(8,128)S(1)}, s32[256,256]{1,0:T(8,128)}, u32[]{:S(2)}) copy-start(s32[256,256]{1,0:T(8,128)} %param.16) | copy-start | bytes 786436
  7.2 8.7 %copy-start = (bf16[256,6144]{1,0:T(8,128)(2,1)S(1)}, bf16[256,6144]{1,0:T(8,128)(2,1)}, u32[]{:S(2)}) copy-start(bf16[256,6144]{1,0:T(8,128)(2,1)} %param.13) | copy-start | bytes 9437188
  7.2 59.8 %all-gather.9.cloned.1.call-start = ((), (), s32[]{:S(2)}) async-start(), calls=%async_computation.3 | async-start | bytes 3342336 | tf_op jit(solution)/shard_map/all_gather | solution.py:41
  7.9 113.4 %all-gather.11.cloned.1.call-start = ((), (), s32[]{:S(2)}) async-start(), calls=%async_computation.4 | async-start | bytes 3342336 | tf_op jit(solution)/shard_map/all_gather | solution.py:40
  8.7 167.1 %all-gather.7.cloned.1.call-start = ((), (), s32[]{:S(2)}) async-start(), calls=%async_computation.2 | async-start | bytes 3342336 | tf_op jit(solution)/shard_map/all_gather | solution.py:42
  9.4 221.2 %all-gather.15.cloned.1.call-start = ((), (), s32[]{:S(2)}) async-start(), calls=%async_computation.6 | async-start | bytes 3342336 | tf_op jit(solution)/shard_map/all_gather | solution.py:43
  11.2 277.7 %all-gather.17.cloned.1.call-start = ((), (), s32[]{:S(2)}) async-start(), calls=%async_computation.7 | async-start | bytes 3342336 | tf_op jit(solution)/shard_map/all_gather | solution.py:54
  11.8 337.0 %all-gather.13.cloned.1.call-start = ((), (), s32[]{:S(2)}) async-start(), calls=%async_computation.5 | async-start | bytes 3342336 | tf_op jit(solution)/shard_map/all_gather | solution.py:55
  13.5 468.8 %all-reduce.3.cloned.1.call-start = ((), (), s32[]{:S(2)}) async-start(), calls=%async_computation.10 | async-start | bytes 12582912 | tf_op jit(solution)/shard_map/psum | solution.py:83
  348.8 3.1 copy-start.1
  348.8 3.1 copy-start.10
  354.6 217.6 %reduce-scatter.3.cloned.1.call-start = ((), (), s32[]{:S(2)}) async-start(), calls=%async_computation.8 | async-start | bytes 3342336 | tf_op jit(solution)/shard_map/reduce_scatter | solution.py:114
  482.4 5.5 copy-start.2
  482.4 5.6 copy-start.4
  492.2 0.9 copy-start.11
  492.2 163.7 %reduce-scatter.5.cloned.1.call-start = ((), (), s32[]{:S(2)}) async-start(), calls=%async_computation.9 | async-start | bytes 3342336 | tf_op jit(solution)/shard_map/reduce_scatter | solution.py:92
  493.1 5.5 copy-start.5
  501.9 1.0 copy-start.8
  501.9 70.3 %copy-start.3 = (f32[384,256]{1,0:T(8,128)S(1)}, f32[384,256]{1,0:T(8,128)}, u32[]{:S(2)}) copy-start(f32[384,256]{1,0:T(8,128)} %param.21) | copy-start | bytes 1179652
  501.9 157.0 %copy-start.12 = (f32[256,384]{1,0:T(8,128)S(1)}, f32[256,384]{1,0:T(8,128)}, u32[]{:S(2)}) copy-start(f32[256,384]{1,0:T(8,128)} %param.24) | copy-start | bytes 1179652
  501.9 235.1 %copy-start.9 = (f32[384,256]{1,0:T(8,128)S(1)}, f32[384,256]{1,0:T(8,128)}, u32[]{:S(2)}) copy-start(f32[384,256]{1,0:T(8,128)} %param.23) | copy-start | bytes 1179652
  572.2 245.0 %copy-start.6 = (bf16[384,256]{1,0:T(8,128)(2,1)S(1)}, bf16[384,256]{1,0:T(8,128)(2,1)}, u32[]{:S(2)}) copy-start(bf16[384,256]{1,0:T(8,128)(2,1)} %reduce-scatter.3.cloned.1.call-done) | copy-start | bytes 589828
  655.9 159.6 %copy-start.7 = (bf16[384,256]{1,0:T(8,128)(2,1)S(1)}, bf16[384,256]{1,0:T(8,128)(2,1)}, u32[]{:S(2)}) copy-start(bf16[384,256]{1,0:T(8,128)(2,1)} %reduce-scatter.5.cloned.1.call-done) | copy-start | bytes 589828
Sparse Core Ops, SparseCore 0:
  10.4 56.4 all-gather.8
  69.4 51.9 all-gather.10
  123.8 51.9 all-gather.6
  178.6 51.9 all-gather.14
  232.8 56.0 all-gather.16
  291.7 57.0 all-gather.12
  354.7 127.6 all-reduce.2
  492.3 79.7 reduce-scatter.2
  575.8 80.0 reduce-scatter.4
where the time goes:
time: 825 us; the launch traced here: 824 us
  waiting for transfers between devices  590 us (72%)
  blocking collectives  150 us (18%)
  matrix products  45.7 us (6%)
  between operations  18.6 us (2%)
  other arithmetic  13.4 us (2%)
    psum x1, waiting for transfers between devices, body(): lax.psum(partial_value.astype(jnp.bfloat16), 'tensor').astype(jnp.float32)  128 us
    reduce_scatter x1, waiting for transfers between devices, body(): lax.psum_scatter(((first + second) * scale_out).astype(jnp.bfloat16), 'dp...  82 us
    psum x1, blocking collectives, body(): lax.psum(jnp.sum(basis_value * curv_value) + jnp.sum(basis_out * curv_out...  77.2 us
    psum x1, blocking collectives, body(): lax.psum(jnp.sum(rest_value * rest_value) + jnp.sum(rest_out * rest_out),...  73.3 us
    reduce_scatter x1, waiting for transfers between devices, body(): lax.psum_scatter((jnp.einsum('ti,ta->ia', normed, value_back, preferred_e...  68.5 us
    all_gather x1, waiting for transfers between devices, body(): lax.all_gather(basis_out.astype(jnp.bfloat16), 'dp', axis=1, tiled=True)  55.4 us
    all_gather x1, waiting for transfers between devices, body(): lax.all_gather(w_out, 'dp', axis=1, tiled=True)  54 us
    all_gather x1, waiting for transfers between devices, body(): lax.all_gather(basis_value_b, 'dp', axis=0, tiled=True)  51.2 us
  transfers between devices with their start and end apart: 9, of which 9 were waited for; matrix products, arithmetic and copies ran while one was open for 5% of the time, Pallas kernels for 0%

commit v1 on v0

--- a/solution.py
+++ b/solution.py
@@ -79,8 +79,9 @@
     tangent_partial = jnp.dot(
         mixed, tangent_out, preferred_element_type=jnp.float32
     ) * scale_out + jnp.dot(tangent_mixed, out_full, preferred_element_type=jnp.float32)
+    _save_pipes = lambda buf: jnp.sum(lax.all_gather(buf, "tensor"), 0)
     attn, tangent_attn = (
-        lax.psum(partial_value.astype(jnp.bfloat16), "tensor").astype(jnp.float32),
+        _save_pipes(partial_value.astype(jnp.bfloat16)).astype(jnp.float32),
         lax.psum(tangent_partial.astype(jnp.bfloat16), "tensor").astype(jnp.float32),
     )
     factor = loss_gain * full_width / total_tokens

time: 825 us -> 1060 us (1.28)
  waiting for transfers between devices: 590 us -> 806 us
  other arithmetic: 13.4 us -> 32.1 us
    all_gather x0 -> x1, waiting for transfers between devices: none -> 250 us  [body(): _save_pipes = lambda buf: jnp.sum(lax.all_gather(buf, 'tensor'), 0)]
    psum x1, waiting for transfers between devices: 128 us -> 93.5 us  [body(): lax.psum(tangent_partial.astype(jnp.bfloat16), 'tensor').astype(jnp.float32)]
    reduce_sum x0 -> x1, other arithmetic: none -> 18.7 us  [body(): _save_pipes = lambda buf: jnp.sum(lax.all_gather(buf, 'tensor'), 0)]
  transfers between devices with their start and end apart: 9 -> 10, of which waited for: 9 -> 10; matrix products, arithmetic and copies ran while one was open for 5% -> 7% of each run, Pallas kernels for 0% -> 0%
where the time goes in v1:
time: 1060 us
  waiting for transfers between devices  806 us (76%)
  blocking collectives  151 us (14%)
  matrix products  49.1 us (5%)
  other arithmetic  32.1 us (3%)
  between operations  19 us (2%)
    all_gather x1, waiting for transfers between devices, body(): _save_pipes = lambda buf: jnp.sum(lax.all_gather(buf, 'tensor'), 0)  250 us
    psum x1, waiting for transfers between devices, body(): lax.psum(tangent_partial.astype(jnp.bfloat16), 'tensor').astype(jnp.float32)  93.5 us
    reduce_scatter x1, waiting for transfers between devices, body(): lax.psum_scatter(((first + second) * scale_out).astype(jnp.bfloat16), 'dp...  82 us
    psum x1, blocking collectives, body(): lax.psum(jnp.sum(basis_value * curv_value) + jnp.sum(basis_out * curv_out...  77.2 us
    psum x1, blocking collectives, body(): lax.psum(jnp.sum(rest_value * rest_value) + jnp.sum(rest_out * rest_out),...  73.4 us
    reduce_scatter x1, waiting for transfers between devices, body(): lax.psum_scatter((jnp.einsum('ti,ta->ia', normed, value_back, preferred_e...  68.4 us
    all_gather x1, waiting for transfers between devices, body(): lax.all_gather(w_out, 'dp', axis=1, tiled=True)  54.7 us
    all_gather x1, waiting for transfers between devices, body(): lax.all_gather(basis_out.astype(jnp.bfloat16), 'dp', axis=1, tiled=True)  54.6 us
  transfers between devices with their start and end apart: 10, of which 10 were waited for; matrix products, arithmetic and copies ran while one was open for 7% of the time, Pallas kernels for 0%

profile of v1, /device:TPU:1, one launch (start us, length us, event | category | flops | bytes accessed | tf_op | source)
XLA Modules:
  0.0 1062.8 jit_solution(3429953072142666800)
XLA Ops:
  7.2 0.7 all-gather.11.cloned.1.call-update
  8.0 0.7 all-gather.13.cloned.1.call-update
  8.7 0.7 all-gather.9.cloned.1.call-update
  9.4 0.5 all-gather.19.cloned.1.call-update
  10.0 1.7 convert_element_type.90
  11.8 1.7 convert_element_type.89
  13.6 2.0 copy.19
  15.9 0.7 fusion.5
  16.6 50.4 %all-gather.11.cloned.1.call-done = bf16[6144,256]{1,0:T(8,128)(2,1)} async-done(((bf16[384,256]{1,0:T(8,128)(2,1)}), bf16[6144,256]{1,0:T(8,128)(2,1)}) %all-gather.11.cloned.1.call-update) | async-done | bytes 3145744 | tf_op jit(solution)/shard_map/all_gather | solution.py:41
  66.9 3.4 convolution_convert_fusion.5
  70.4 51.0 %all-gather.13.cloned.1.call-done = bf16[6144,256]{1,0:T(8,128)(2,1)} async-done(((bf16[384,256]{1,0:T(8,128)(2,1)}), bf16[6144,256]{1,0:T(8,128)(2,1)}) %all-gather.13.cloned.1.call-update) | async-done | bytes 3145744 | tf_op jit(solution)/shard_map/all_gather | solution.py:40
  121.3 3.4 convolution_convert_fusion.4
  124.8 2.2 fusion.34
  127.0 1.1 divide_convert_fusion
  128.0 47.7 %all-gather.9.cloned.1.call-done = bf16[6144,256]{1,0:T(8,128)(2,1)} async-done(((bf16[384,256]{1,0:T(8,128)(2,1)}), bf16[6144,256]{1,0:T(8,128)(2,1)}) %all-gather.9.cloned.1.call-update) | async-done | bytes 3145744 | tf_op jit(solution)/shard_map/all_gather | solution.py:42
  175.8 3.4 convolution_convert_fusion.6
  179.2 0.2 convolution_convert_fusion.3
  179.4 54.7 %all-gather.19.cloned.1.call-done = bf16[256,6144]{1,0:T(8,128)(2,1)} async-done(((bf16[256,384]{1,0:T(8,128)(2,1)}), bf16[256,6144]{1,0:T(8,128)(2,1)}) %all-gather.19.cloned.1.call-update) | async-done | bytes 3145744 | tf_op jit(solution)/shard_map/all_gather | solution.py:54
  234.0 4.5 convolution_convert_fusion
  238.6 51.3 %all-gather.17.cloned.1.call-done = bf16[6144,256]{1,0:T(8,128)(2,1)} async-done(((bf16[384,256]{1,0:T(8,128)(2,1)}), bf16[6144,256]{1,0:T(8,128)(2,1)}) %all-gather.17.cloned.1.call-update) | async-done | bytes 3145744 | tf_op jit(solution)/shard_map/all_gather | solution.py:43
  289.9 3.4 fusion.18
  293.3 0.8 convolution_convert_fusion.2
  294.2 54.6 %all-gather.15.cloned.1.call-done = bf16[256,6144]{1,0:T(8,128)(2,1)} async-done(((bf16[256,384]{1,0:T(8,128)(2,1)}), bf16[256,6144]{1,0:T(8,128)(2,1)}) %all-gather.15.cloned.1.call-update) | async-done | bytes 3145744 | tf_op jit(solution)/shard_map/all_gather | solution.py:55
  348.8 3.0 convolution_multiply_fusion.1
  351.8 2.7 fusion.3
  354.5 0.2 reduce-scatter.3.cloned.1.call-start
  354.8 250.0 %all-gather.21.cloned.1.call-done = bf16[4096,6144]{1,0:T(8,128)(2,1)} async-done(((bf16[256,6144]{1,0:T(8,128)(2,1)}), bf16[4096,6144]{1,0:T(8,128)(2,1)}) %all-gather.21.cloned.1.call-update) | async-done | bytes 50331664 | tf_op jit(solution)/shard_map/all_gather | solution.py:82
  604.8 18.7 %reduce_sum.68 = bf16[256,6144]{1,0:T(8,128)(2,1)} reduce(bf16[16,256,6144]{2,1,0:T(8,128)(2,1)} %bitcast.59, bf16[]{:T(256)} %constant.30.clone.1), dimensions={0}, to_apply=%region_4.5 | reduce | flops 23592960 | bytes 53477376 | tf_op jit(solution)/shard_map/reduce_sum | solution.py:82
  623.5 6.2 convolution_multiply_fusion.3
  629.6 93.5 %all-reduce.2.cloned.1.call-done = bf16[256,6144]{1,0:T(8,128)(2,1)} async-done(((bf16[256,6144]{1,0:T(8,128)(2,1)}), bf16[256,6144]{1,0:T(8,128)(2,1)}) %all-reduce.2.cloned.1.call-update) | async-done | bytes 3145744 | tf_op jit(solution)/shard_map/psum | solution.py:85
  723.2 3.9 fusion.17
  727.0 0.2 convolution_convert_fusion.1
  727.3 3.0 fusion.4
  730.3 0.8 copy-done.9
  731.1 5.5 fusion.26
  736.7 3.2 fusion.2
  739.9 1.0 copy-done.6
  741.7 68.4 %reduce-scatter.3.cloned.1.call-done = bf16[384,256]{1,0:T(8,128)(2,1)} async-done(((bf16[6144,256]{1,0:T(8,128)(2,1)}), bf16[384,256]{1,0:T(8,128)(2,1)}) %reduce-scatter.3.cloned.1.call-update) | async-done | bytes 196624 | tf_op jit(solution)/shard_map/reduce_scatter | solution.py:115
  810.1 1.7 fusion.19
  811.8 82.0 %reduce-scatter.5.cloned.1.call-done = bf16[384,256]{1,0:T(8,128)(2,1)} async-done(((bf16[6144,256]{1,0:T(8,128)(2,1)}), bf16[384,256]{1,0:T(8,128)(2,1)}) %reduce-scatter.5.cloned.1.call-update) | async-done | bytes 196624 | tf_op jit(solution)/shard_map/reduce_scatter | solution.py:93
  893.8 1.7 fusion.21
  897.0 77.2 %psum.22 = f32[]{:T(128)} all-reduce(f32[]{:T(128)S(6)} %add.52), channel_id=1, replica_groups=mesh['dp'=16,'tensor'=16] {'dp','tensor'}, use_global_device_ids=true, to_apply=%region_9.10 | all-reduce | flops 1 | bytes 8 | tf_op jit(solution)/shard_map/psum | solution.py:126
  974.9 1.6 multiply_reduce_fusion.1
  976.5 1.6 multiply_reduce_fusion
  979.4 73.4 %psum.23 = f32[]{:T(128)} all-reduce(f32[]{:T(128)S(6)} %add.53), channel_id=1, replica_groups=mesh['dp'=16,'tensor'=16] {'dp','tensor'}, use_global_device_ids=true, to_apply=%region_12.13 | all-reduce | flops 1 | bytes 8 | tf_op jit(solution)/shard_map/psum | solution.py:134
  1053.6 0.9 copy.26
  1054.5 0.6 pad_maximum_fusion
  1055.1 0.8 broadcast_divide_fusion.1
  (43 shorter events, 1.1 us)
Async XLA Ops:
  7.2 8.4 copy-start.11
  7.2 8.7 copy-start
  7.2 59.8 %all-gather.11.cloned.1.call-start = ((), (), s32[]{:S(2)}) async-start(), calls=%async_computation.3 | async-start | bytes 3342336 | tf_op jit(solution)/shard_map/all_gather | solution.py:41
  7.9 113.4 %all-gather.13.cloned.1.call-start = ((), (), s32[]{:S(2)}) async-start(), calls=%async_computation.4 | async-start | bytes 3342336 | tf_op jit(solution)/shard_map/all_gather | solution.py:40
  8.7 167.1 %all-gather.9.cloned.1.call-start = ((), (), s32[]{:S(2)}) async-start(), calls=%async_computation.2 | async-start | bytes 3342336 | tf_op jit(solution)/shard_map/all_gather | solution.py:42
  9.4 224.6 %all-gather.19.cloned.1.call-start = ((), (), s32[]{:S(2)}) async-start(), calls=%async_computation.7 | async-start | bytes 3342336 | tf_op jit(solution)/shard_map/all_gather | solution.py:54
  10.0 279.9 %all-gather.17.cloned.1.call-start = ((), (), s32[]{:S(2)}) async-start(), calls=%async_computation.6 | async-start | bytes 3342336 | tf_op jit(solution)/shard_map/all_gather | solution.py:43
  11.7 337.0 %all-gather.15.cloned.1.call-start = ((), (), s32[]{:S(2)}) async-start(), calls=%async_computation.5 | async-start | bytes 3342336 | tf_op jit(solution)/shard_map/all_gather | solution.py:55
  13.5 591.3 %all-gather.21.cloned.1.call-start = ((), (), s32[]{:S(2)}) async-start(), calls=%async_computation.11 | async-start | bytes 53477376 | tf_op jit(solution)/shard_map/all_gather | solution.py:82
  238.6 484.6 %all-reduce.2.cloned.1.call-start = ((), (), s32[]{:S(2)}) async-start(), calls=%async_computation.8 | async-start | bytes 6291456 | tf_op jit(solution)/shard_map/psum | solution.py:85
  348.8 3.1 copy-start.1
  348.8 3.1 copy-start.8
  354.5 455.6 %reduce-scatter.3.cloned.1.call-start = ((), (), s32[]{:S(2)}) async-start(), calls=%async_computation.9 | async-start | bytes 3342336 | tf_op jit(solution)/shard_map/reduce_scatter | solution.py:115
  730.2 0.9 copy-start.9
  730.3 163.6 %reduce-scatter.5.cloned.1.call-start = ((), (), s32[]{:S(2)}) async-start(), calls=%async_computation.10 | async-start | bytes 3342336 | tf_op jit(solution)/shard_map/reduce_scatter | solution.py:93
  731.1 5.5 copy-start.3
  739.9 1.0 copy-start.6
  739.9 70.2 %copy-start.2 = (f32[384,256]{1,0:T(8,128)S(1)}, f32[384,256]{1,0:T(8,128)}, u32[]{:S(2)}) copy-start(f32[384,256]{1,0:T(8,128)} %param.21) | copy-start | bytes 1179652
  739.9 156.9 %copy-start.10 = (f32[256,384]{1,0:T(8,128)S(1)}, f32[256,384]{1,0:T(8,128)}, u32[]{:S(2)}) copy-start(f32[256,384]{1,0:T(8,128)} %param.24) | copy-start | bytes 1179652
  739.9 234.9 %copy-start.7 = (f32[384,256]{1,0:T(8,128)S(1)}, f32[384,256]{1,0:T(8,128)}, u32[]{:S(2)}) copy-start(f32[384,256]{1,0:T(8,128)} %param.23) | copy-start | bytes 1179652
  810.1 245.0 %copy-start.4 = (bf16[384,256]{1,0:T(8,128)(2,1)S(1)}, bf16[384,256]{1,0:T(8,128)(2,1)}, u32[]{:S(2)}) copy-start(bf16[384,256]{1,0:T(8,128)(2,1)} %reduce-scatter.3.cloned.1.call-done) | copy-start | bytes 589828
  893.8 159.7 %copy-start.5 = (bf16[384,256]{1,0:T(8,128)(2,1)S(1)}, bf16[384,256]{1,0:T(8,128)(2,1)}, u32[]{:S(2)}) copy-start(bf16[384,256]{1,0:T(8,128)(2,1)} %reduce-scatter.5.cloned.1.call-done) | copy-start | bytes 589828
Sparse Core Ops, SparseCore 0:
  10.4 56.4 all-gather.10
  69.4 51.9 all-gather.12
  123.8 51.9 all-gather.8
  178.0 55.9 all-gather.18
  236.9 52.9 all-gather.16
  292.7 55.9 all-gather.14
  350.6 254.1 all-gather.20
  607.2 115.9 all-reduce.1
  730.4 79.6 reduce-scatter.2
  813.6 80.1 reduce-scatter.4
